TPU v7x, 32 devices: a whole 2x2x4 slice. The times are simulated.
32 devices in a mesh: grp: 2 (over x), chan: 16 (over z, y, core).
Axes of the slice: x: 2, y: 2, z: 4, core: 2. Of those that a mesh axis runs over, the one named last changes fastest.
Arguments:
- voltages: bfloat16 [4096, 64, 512], P('chan', 'grp'), parts along dimension 1, may hold values from -6 to 6
- exponents: int32 [64], P('grp'), parts along dimension 0, may hold values from 0 to 2, as said below
- pairs: int32 [128, 2], replicated, may hold values from 0 to 31, as said below
Outputs:
- visibilities: bfloat16 [64, 128, 2, 128, 128], P(('grp', 'chan')), parts along dimension 0
There are 2 independent parts, one for each index of `grp`. A program takes and returns all parts, laid end to end along the dimension named above; an argument that names none is the same for every part. Nothing has to cross between parts.
Inputs may be any that keep to these rules, and one draw needn't show every extreme that they name: exponents are whole numbers. The 128 pairs are distinct and each has first member at most its second.
All inputs are finite; a program needn't handle non-finite values.
Results may differ from a plain program's by a relative error of at most 0.001.
Values may be sent and summed in bfloat16 or wider, within the bound.
A program may use at most 192 MiB of HBM per device.

v0:
```python
import jax
import jax.numpy as jnp
from jax import lax
from jax.sharding import PartitionSpec as P

PANEL = 128
NT = 256


def correlate_plane(plane, pairs):
    width = plane.shape[1]
    half = width // 2
    count = plane.shape[0] // PANEL
    panels = plane.reshape(count, PANEL, width)
    group_size = 32
    groups = pairs.reshape(-1, group_size, 2)
    labels = jnp.arange(count, dtype=jnp.int32)

    def select(which):
        onehot = (which[:, None] == labels[None, :]).astype(jnp.bfloat16)
        picked = jnp.einsum("kn,nix->kix", onehot, panels, preferred_element_type=jnp.float32)
        return picked.astype(jnp.bfloat16).reshape(group_size, PANEL, 2, half)

    def one_group(chosen):
        left = select(chosen[:, 0])
        right = select(chosen[:, 1])
        quads = jnp.einsum("kiat,kjbt->kabij", left, right, preferred_element_type=jnp.float32)
        real_part = quads[:, 0, 0] + quads[:, 1, 1]
        imag_part = quads[:, 1, 0] - quads[:, 0, 1]
        return jnp.stack([real_part, imag_part], axis=1)

    return lax.map(one_group, groups).reshape(-1, 2, PANEL, PANEL)


def correlate_channels(turned, pairs):

    def one_channel(plane):
        return correlate_plane(plane, pairs)

    return lax.map(one_channel, jnp.moveaxis(turned, 1, 0))


def input_power(turned):
    wide = turned.astype(jnp.float32)
    return jnp.sum(wide * wide, axis=(1, 2))


def on_device(voltages, exponents, pairs):
    gain = jnp.exp2(-exponents.astype(jnp.float32)).astype(jnp.bfloat16)
    scaled = voltages * gain[None, :, None]
    total_samples = exponents.shape[0] * NT
    power = lax.all_gather(input_power(scaled), "chan", axis=0, tiled=True)
    turned = lax.all_to_all(scaled, "chan", split_axis=1, concat_axis=0, tiled=True)
    raw = correlate_channels(turned, pairs)
    mean_power = power / total_samples
    rows = mean_power.reshape(-1, PANEL)
    left_power = jnp.take(rows, pairs[:, 0], axis=0)
    right_power = jnp.take(rows, pairs[:, 1], axis=0)
    denom = jnp.sqrt(NT * left_power[:, :, None] * right_power[:, None, :])
    return (raw / denom[None, :, None, :, :]).astype(jnp.bfloat16)


def solution(mesh):
    return jax.shard_map(
        on_device,
        mesh=mesh,
        in_specs=(P("chan", "grp", None), P("grp"), P()),
        out_specs=P(("grp", "chan"), None, None, None, None),
        check_vma=False,
    )
```

profile of v0, /device:TPU:11, one launch (start us, length us, event | category | flops | bytes accessed | tf_op | source)
XLA Modules:
  0.0 683.6 jit_solution(13939410700513925443)
XLA Ops:
  0.7 9.6 %multiply_reduce_fusion = (f32[256]{0:T(256)S(1)}, bf16[256,32,512]{2,0,1:T(8,128)(2,1)}) fusion(bf16[32]{0:T(256)(128)(2,1)S(1)} %exponential_convert_fusion, bf16[256,32,512]{2,1,0:T(8,128)(2,1)} %param.9), kind=kLoop, calls=%fused_computation.29 | loop fusion | flops 16776960 | bytes 16778304 | tf_op jit(solution)/shard_map/reduce_sum | solution.py:45
  17.1 192.6 %all-gather = f32[16,1,256]{2,1,0:T(1,128)S(1)} all-gather(f32[1,1,256]{2,1,0:T(1,128)S(1)} %bitcast.99), channel_id=1, replica_groups=mesh['grp'=2,'chan'=16] {'chan'}, dimensions={0}, use_global_device_ids=true | all-gather | bytes 17408 | tf_op jit(solution)/shard_map/all_gather | solution.py:52
  215.7 7.5 %copy.26 = bf16[16,256,2,512]{3,1,0,2:T(8,128)(2,1)} copy(bf16[16,256,2,512]{3,1,2,0:T(8,128)(2,1)} %bitcast.3) | data formatting | bytes 16777216 | tf_op jit(solution)/shard_map/all_to_all | solution.py:53
  223.2 440.5 %while.23 = (s32[]{:T(128)}, f32[2,128,2,128,128]{4,3,2,1,0:T(8,128)}, s32[128,2]{0,1:T(2,128)S(1)}, bf16[2,4096,512]{2,1,0:T(8,128)(2,1)}, s32[]{:T(128)}, /*index=5*/s32[]{:T(128)}, s32[]{:T(128)}) while((s32[]{:T(128)}, f32[2,128,2,128,128]{4,3,2,1,0:T(8,128)}, s32[128,2]{0,1:T(2,128)S(1)}, bf16[2,4096,512]{2,1,0:T(8,128)(2,1)}, s32[]{:T(128)}, ...), condition=%wide.region_3.4_spmd, body=%wide.region_0.3_spmd.sunk | while | flops 1348470784 | bytes 138415600 | solution.py:40
  230.2 201.7 %while.24 = (s32[]{:T(128)}, f32[4,32,2,128,128]{4,3,2,1,0:T(8,128)}, s32[4,32,2]{1,0,2:T(4,128)S(1)}, bf16[32,128,512]{2,0,1:T(8,128)(2,1)}, s32[]{:T(128)}) while((s32[]{:T(128)}, f32[4,32,2,128,128]{4,3,2,1,0:T(8,128)}, s32[4,32,2]{1,0,2:T(4,128)S(1)}, bf16[32,128,512]{2,0,1:T(8,128)(2,1)}, s32[]{:T(128)}) %tuple.52), condition=%wide.region_2.2_spmd.clone.clone, body=%wide.region_1.1_spmd.clone.clone.sunk | while | flops 1348470784 | bytes 88081744 | solution.py:32
  235.6 6.9 %reshape.106 = bf16[32,128,2,256]{3,2,0,1:T(2,128)(2,1)} reshape(bf16[32,128,512]{2,0,1:T(8,128)(2,1)} %convolution_convert_fusion.4) | data formatting | bytes 8388608 | tf_op jit(solution)/shard_map/while/body/eval_jaxpr/while/body/eval_jaxpr/reshape | solution.py:22
  248.0 6.9 %reshape.107 = bf16[32,128,2,256]{3,2,0,1:T(2,128)(2,1)} reshape(bf16[32,128,512]{2,0,1:T(8,128)(2,1)} %convolution_convert_fusion.5) | data formatting | bytes 8388608 | tf_op jit(solution)/shard_map/while/body/eval_jaxpr/while/body/eval_jaxpr/reshape | solution.py:22
  254.9 12.5 %fusion.36 = f32[32,2,2,128,128]{3,4,1,2,0:T(8,128)S(1)} fusion(bf16[32,128,2,256,1]{3,2,0,1,4:T(2,128)(2,1)} %bitcast.91, bf16[32,128,2,256,1]{3,2,0,1,4:T(2,128)(2,1)} %bitcast.92), kind=kOutput, calls=%fused_computation.7.clone.1 | convolution fusion | flops 1073741824 | bytes 16777216 | tf_op jit(solution)/shard_map/while/body/eval_jaxpr/while/body/eval_jaxpr/kiat,kjbt->kabij/dot_general | solution.py:27
  286.0 6.9 %reshape.106 = bf16[32,128,2,256]{3,2,0,1:T(2,128)(2,1)} reshape(bf16[32,128,512]{2,0,1:T(8,128)(2,1)} %convolution_convert_fusion.4) | data formatting | bytes 8388608 | tf_op jit(solution)/shard_map/while/body/eval_jaxpr/while/body/eval_jaxpr/reshape | solution.py:22
  298.4 6.9 %reshape.107 = bf16[32,128,2,256]{3,2,0,1:T(2,128)(2,1)} reshape(bf16[32,128,512]{2,0,1:T(8,128)(2,1)} %convolution_convert_fusion.5) | data formatting | bytes 8388608 | tf_op jit(solution)/shard_map/while/body/eval_jaxpr/while/body/eval_jaxpr/reshape | solution.py:22
  305.3 12.5 %fusion.36 = f32[32,2,2,128,128]{3,4,1,2,0:T(8,128)S(1)} fusion(bf16[32,128,2,256,1]{3,2,0,1,4:T(2,128)(2,1)} %bitcast.91, bf16[32,128,2,256,1]{3,2,0,1,4:T(2,128)(2,1)} %bitcast.92), kind=kOutput, calls=%fused_computation.7.clone.1 | convolution fusion | flops 1073741824 | bytes 16777216 | tf_op jit(solution)/shard_map/while/body/eval_jaxpr/while/body/eval_jaxpr/kiat,kjbt->kabij/dot_general | solution.py:27
  336.4 6.9 %reshape.106 = bf16[32,128,2,256]{3,2,0,1:T(2,128)(2,1)} reshape(bf16[32,128,512]{2,0,1:T(8,128)(2,1)} %convolution_convert_fusion.4) | data formatting | bytes 8388608 | tf_op jit(solution)/shard_map/while/body/eval_jaxpr/while/body/eval_jaxpr/reshape | solution.py:22
  348.8 6.9 %reshape.107 = bf16[32,128,2,256]{3,2,0,1:T(2,128)(2,1)} reshape(bf16[32,128,512]{2,0,1:T(8,128)(2,1)} %convolution_convert_fusion.5) | data formatting | bytes 8388608 | tf_op jit(solution)/shard_map/while/body/eval_jaxpr/while/body/eval_jaxpr/reshape | solution.py:22
  355.7 12.5 %fusion.36 = f32[32,2,2,128,128]{3,4,1,2,0:T(8,128)S(1)} fusion(bf16[32,128,2,256,1]{3,2,0,1,4:T(2,128)(2,1)} %bitcast.91, bf16[32,128,2,256,1]{3,2,0,1,4:T(2,128)(2,1)} %bitcast.92), kind=kOutput, calls=%fused_computation.7.clone.1 | convolution fusion | flops 1073741824 | bytes 16777216 | tf_op jit(solution)/shard_map/while/body/eval_jaxpr/while/body/eval_jaxpr/kiat,kjbt->kabij/dot_general | solution.py:27
  386.9 6.9 %reshape.106 = bf16[32,128,2,256]{3,2,0,1:T(2,128)(2,1)} reshape(bf16[32,128,512]{2,0,1:T(8,128)(2,1)} %convolution_convert_fusion.4) | data formatting | bytes 8388608 | tf_op jit(solution)/shard_map/while/body/eval_jaxpr/while/body/eval_jaxpr/reshape | solution.py:22
  399.2 6.9 %reshape.107 = bf16[32,128,2,256]{3,2,0,1:T(2,128)(2,1)} reshape(bf16[32,128,512]{2,0,1:T(8,128)(2,1)} %convolution_convert_fusion.5) | data formatting | bytes 8388608 | tf_op jit(solution)/shard_map/while/body/eval_jaxpr/while/body/eval_jaxpr/reshape | solution.py:22
  406.1 12.5 %fusion.36 = f32[32,2,2,128,128]{3,4,1,2,0:T(8,128)S(1)} fusion(bf16[32,128,2,256,1]{3,2,0,1,4:T(2,128)(2,1)} %bitcast.91, bf16[32,128,2,256,1]{3,2,0,1,4:T(2,128)(2,1)} %bitcast.92), kind=kOutput, calls=%fused_computation.7.clone.1 | convolution fusion | flops 1073741824 | bytes 16777216 | tf_op jit(solution)/shard_map/while/body/eval_jaxpr/while/body/eval_jaxpr/kiat,kjbt->kabij/dot_general | solution.py:27
  431.8 11.6 %bitcast_dynamic-update-slice_fusion.2 = f32[2,128,2,128,128]{4,3,2,1,0:T(8,128)} fusion(f32[2,128,2,128,128]{4,3,2,1,0:T(8,128)} %get-tuple-element.207, s32[]{:T(128)S(6)} %copy.66, f32[1,128,2,128,128]{4,3,2,1,0:T(8,128)} %bitcast.93), kind=kLoop, calls=%fused_computation.26.clone.1 | loop fusion | bytes 33554436 | tf_op jit(solution)/shard_map/while/body/jit(dynamic_update_index_in_dim)/dynamic_update_slice | solution.py:40
  450.5 201.6 %while.24 = (s32[]{:T(128)}, f32[4,32,2,128,128]{4,3,2,1,0:T(8,128)}, s32[4,32,2]{1,0,2:T(4,128)S(1)}, bf16[32,128,512]{2,0,1:T(8,128)(2,1)}, s32[]{:T(128)}) while((s32[]{:T(128)}, f32[4,32,2,128,128]{4,3,2,1,0:T(8,128)}, s32[4,32,2]{1,0,2:T(4,128)S(1)}, bf16[32,128,512]{2,0,1:T(8,128)(2,1)}, s32[]{:T(128)}) %tuple.52), condition=%wide.region_2.2_spmd.clone.clone, body=%wide.region_1.1_spmd.clone.clone.sunk | while | flops 1348470784 | bytes 88081744 | solution.py:32
  455.9 6.9 %reshape.106 = bf16[32,128,2,256]{3,2,0,1:T(2,128)(2,1)} reshape(bf16[32,128,512]{2,0,1:T(8,128)(2,1)} %convolution_convert_fusion.4) | data formatting | bytes 8388608 | tf_op jit(solution)/shard_map/while/body/eval_jaxpr/while/body/eval_jaxpr/reshape | solution.py:22
  468.3 6.9 %reshape.107 = bf16[32,128,2,256]{3,2,0,1:T(2,128)(2,1)} reshape(bf16[32,128,512]{2,0,1:T(8,128)(2,1)} %convolution_convert_fusion.5) | data formatting | bytes 8388608 | tf_op jit(solution)/shard_map/while/body/eval_jaxpr/while/body/eval_jaxpr/reshape | solution.py:22
  475.1 12.5 %fusion.36 = f32[32,2,2,128,128]{3,4,1,2,0:T(8,128)S(1)} fusion(bf16[32,128,2,256,1]{3,2,0,1,4:T(2,128)(2,1)} %bitcast.91, bf16[32,128,2,256,1]{3,2,0,1,4:T(2,128)(2,1)} %bitcast.92), kind=kOutput, calls=%fused_computation.7.clone.1 | convolution fusion | flops 1073741824 | bytes 16777216 | tf_op jit(solution)/shard_map/while/body/eval_jaxpr/while/body/eval_jaxpr/kiat,kjbt->kabij/dot_general | solution.py:27
  506.3 6.9 %reshape.106 = bf16[32,128,2,256]{3,2,0,1:T(2,128)(2,1)} reshape(bf16[32,128,512]{2,0,1:T(8,128)(2,1)} %convolution_convert_fusion.4) | data formatting | bytes 8388608 | tf_op jit(solution)/shard_map/while/body/eval_jaxpr/while/body/eval_jaxpr/reshape | solution.py:22
  518.7 6.9 %reshape.107 = bf16[32,128,2,256]{3,2,0,1:T(2,128)(2,1)} reshape(bf16[32,128,512]{2,0,1:T(8,128)(2,1)} %convolution_convert_fusion.5) | data formatting | bytes 8388608 | tf_op jit(solution)/shard_map/while/body/eval_jaxpr/while/body/eval_jaxpr/reshape | solution.py:22
  525.5 12.5 %fusion.36 = f32[32,2,2,128,128]{3,4,1,2,0:T(8,128)S(1)} fusion(bf16[32,128,2,256,1]{3,2,0,1,4:T(2,128)(2,1)} %bitcast.91, bf16[32,128,2,256,1]{3,2,0,1,4:T(2,128)(2,1)} %bitcast.92), kind=kOutput, calls=%fused_computation.7.clone.1 | convolution fusion | flops 1073741824 | bytes 16777216 | tf_op jit(solution)/shard_map/while/body/eval_jaxpr/while/body/eval_jaxpr/kiat,kjbt->kabij/dot_general | solution.py:27
  556.7 6.9 %reshape.106 = bf16[32,128,2,256]{3,2,0,1:T(2,128)(2,1)} reshape(bf16[32,128,512]{2,0,1:T(8,128)(2,1)} %convolution_convert_fusion.4) | data formatting | bytes 8388608 | tf_op jit(solution)/shard_map/while/body/eval_jaxpr/while/body/eval_jaxpr/reshape | solution.py:22
  569.1 6.9 %reshape.107 = bf16[32,128,2,256]{3,2,0,1:T(2,128)(2,1)} reshape(bf16[32,128,512]{2,0,1:T(8,128)(2,1)} %convolution_convert_fusion.5) | data formatting | bytes 8388608 | tf_op jit(solution)/shard_map/while/body/eval_jaxpr/while/body/eval_jaxpr/reshape | solution.py:22
  575.9 12.5 %fusion.36 = f32[32,2,2,128,128]{3,4,1,2,0:T(8,128)S(1)} fusion(bf16[32,128,2,256,1]{3,2,0,1,4:T(2,128)(2,1)} %bitcast.91, bf16[32,128,2,256,1]{3,2,0,1,4:T(2,128)(2,1)} %bitcast.92), kind=kOutput, calls=%fused_computation.7.clone.1 | convolution fusion | flops 1073741824 | bytes 16777216 | tf_op jit(solution)/shard_map/while/body/eval_jaxpr/while/body/eval_jaxpr/kiat,kjbt->kabij/dot_general | solution.py:27
  607.1 6.9 %reshape.106 = bf16[32,128,2,256]{3,2,0,1:T(2,128)(2,1)} reshape(bf16[32,128,512]{2,0,1:T(8,128)(2,1)} %convolution_convert_fusion.4) | data formatting | bytes 8388608 | tf_op jit(solution)/shard_map/while/body/eval_jaxpr/while/body/eval_jaxpr/reshape | solution.py:22
  626.3 12.5 %fusion.36 = f32[32,2,2,128,128]{3,4,1,2,0:T(8,128)S(1)} fusion(bf16[32,128,2,256,1]{3,2,0,1,4:T(2,128)(2,1)} %bitcast.91, bf16[32,128,2,256,1]{3,2,0,1,4:T(2,128)(2,1)} %bitcast.92), kind=kOutput, calls=%fused_computation.7.clone.1 | convolution fusion | flops 1073741824 | bytes 16777216 | tf_op jit(solution)/shard_map/while/body/eval_jaxpr/while/body/eval_jaxpr/kiat,kjbt->kabij/dot_general | solution.py:27
  652.1 11.6 %bitcast_dynamic-update-slice_fusion.2 = f32[2,128,2,128,128]{4,3,2,1,0:T(8,128)} fusion(f32[2,128,2,128,128]{4,3,2,1,0:T(8,128)} %get-tuple-element.207, s32[]{:T(128)S(6)} %copy.66, f32[1,128,2,128,128]{4,3,2,1,0:T(8,128)} %bitcast.93), kind=kLoop, calls=%fused_computation.26.clone.1 | loop fusion | bytes 33554436 | tf_op jit(solution)/shard_map/while/body/jit(dynamic_update_index_in_dim)/dynamic_update_slice | solution.py:40
  663.7 19.9 %divide_convert_fusion = bf16[2,128,2,128,128]{4,3,2,1,0:T(8,128)(2,1)} fusion(f32[2,128,2,128,128]{4,3,2,1,0:T(8,128)} %get-tuple-element.58, f32[128,128,128]{2,1,0:T(8,128)} %multiply_sqrt_fusion), kind=kLoop, calls=%fused_computation.28 | loop fusion | flops 16777216 | bytes 58720256 | tf_op jit(solution)/shard_map/convert_element_type | solution.py:60
  (95 shorter events, 226.6 us)
Async XLA Ops:
  10.3 199.4 %copy-start = (s32[128,2]{0,1:T(2,128)S(1)}, s32[128,2]{0,1:T(2,128)}, u32[]{:S(2)}) copy-start(s32[128,2]{0,1:T(2,128)} %param.11) | copy-start | bytes 3076
  10.3 205.4 %all-to-all-start = ((bf16[256,32,512]{2,0,1:T(8,128)(2,1)}), bf16[256,32,512]{2,0,1:T(8,128)(2,1)}, u32[]{:S(2)}, u32[]{:S(2)}) async-start(bf16[256,32,512]{2,0,1:T(8,128)(2,1)} %get-tuple-element.112), calls=%async_computation | async-start | bytes 16777216 | tf_op jit(solution)/shard_map/all_to_all | solution.py:53
where the time goes:
time: 688 us; the launch traced here: 684 us
  local copies, waits for them, and re-layouts  239 us (35%)
  blocking collectives  193 us (28%)
  matrix products  187 us (27%)
  other arithmetic  57.9 us (8%)
    all_gather x1, blocking collectives, on_device(): power = lax.all_gather(input_power(scaled), 'chan', axis=0, tiled=True)  193 us
    reshape x16, local copies, waits for them, and re-layouts, select(): return picked.astype(jnp.bfloat16).reshape(group_size, PANEL, 2, half)  111 us
    dot_general x8, matrix products, one_group(): jnp.einsum('kiat,kjbt->kabij', left, right, preferred_element_type=jnp.fl...  100 us
    dot_general x16, matrix products, select(): jnp.einsum('kn,nix->kix', onehot, panels, preferred_element_type=jnp.floa...  86.8 us
    dynamic_update_slice x16, local copies, waits for them, and re-layouts, correlate_plane(): return lax.map(one_group, groups).reshape(-1, 2, PANEL, PANEL)  82.5 us
    dynamic_update_slice x2, local copies, waits for them, and re-layouts, correlate_channels(): return lax.map(one_channel, jnp.moveaxis(turned, 1, 0))  23.3 us
    convert_element_type x1, other arithmetic, on_device(): return (raw / denom[None, :, None, :, :]).astype(jnp.bfloat16)  19.9 us
    broadcast_in_dim x8, other arithmetic, correlate_plane(): return lax.map(one_group, groups).reshape(-1, 2, PANEL, PANEL)  18 us
  transfers between devices with their start and end apart: 1, of which 0 were waited for; matrix products, arithmetic and copies ran while one was open for 1% of the time, Pallas kernels for 0%

commit v1 on v0

--- a/solution.py
+++ b/solution.py
@@ -49,7 +49,32 @@
     gain = jnp.exp2(-exponents.astype(jnp.float32)).astype(jnp.bfloat16)
     scaled = voltages * gain[None, :, None]
     total_samples = exponents.shape[0] * NT
-    power = lax.all_gather(input_power(scaled), "chan", axis=0, tiled=True)
+
+    def mix_the_face(xs, across, dim_at):
+        chunks = []
+        jj = 0
+        z, current_value, out_arr = (
+            lax.axis_size(across),
+            lax.axis_index(across),
+            xs.shape[dim_at],
+        )
+        while jj < z:
+            chunks.append((jj, (jj + 1) % z))
+            jj += 1
+        right_arr = jnp.zeros((*xs.shape[:dim_at], z * out_arr, *xs.shape[dim_at + 1 :]), xs.dtype)
+        far_arr = xs
+        i0 = 0
+        while i0 < z:
+            mixed_arr = (current_value - i0) % z
+            right_arr = lax.dynamic_update_slice_in_dim(
+                right_arr, far_arr, mixed_arr * out_arr, axis=dim_at
+            )
+            if i0 < z - 1:
+                far_arr = lax.ppermute(far_arr, across, perm=chunks)
+            i0 += 1
+        return right_arr
+
+    power = mix_the_face(input_power(scaled), "chan", 0)
     turned = lax.all_to_all(scaled, "chan", split_axis=1, concat_axis=0, tiled=True)
     raw = correlate_channels(turned, pairs)
     mean_power = power / total_samples

time: 688 us -> 733 us (1.065)
  blocking collectives: 193 us -> 0 us
  waiting for transfers between devices: 0.01 us -> 144 us
  starting transfers between devices: 6.74 us -> 92.1 us
    all_gather x1 -> x0, blocking collectives: 193 us -> none  [on_device(): power = lax.all_gather(input_power(scaled), 'chan', axis=0, tiled=True)]
    ppermute x0 -> x15, waiting for transfers between devices: none -> 144 us  [mix_the_face(): far_arr = lax.ppermute(far_arr, across, perm=chunks)]
    ppermute x0 -> x15, starting transfers between devices: none -> 85.3 us  [mix_the_face(): far_arr = lax.ppermute(far_arr, across, perm=chunks)]
  transfers between devices with their start and end apart: 1 -> 16, of which waited for: 0 -> 14; matrix products, arithmetic and copies ran while one was open for 1% -> 1% of each run, Pallas kernels for 0% -> 0%
where the time goes in v1:
time: 733 us; the launch traced here: 724 us
  local copies, waits for them, and re-layouts  243 us (33%)
  matrix products  187 us (26%)
  waiting for transfers between devices  144 us (20%)
  starting transfers between devices  92.1 us (13%)
  other arithmetic  58.1 us (8%)
    ppermute x15, waiting for transfers between devices, mix_the_face(): far_arr = lax.ppermute(far_arr, across, perm=chunks)  144 us
    reshape x16, local copies, waits for them, and re-layouts, select(): return picked.astype(jnp.bfloat16).reshape(group_size, PANEL, 2, half)  111 us
    dot_general x8, matrix products, one_group(): jnp.einsum('kiat,kjbt->kabij', left, right, preferred_element_type=jnp.fl...  100 us
    dot_general x16, matrix products, select(): jnp.einsum('kn,nix->kix', onehot, panels, preferred_element_type=jnp.floa...  86.9 us
    ppermute x15, starting transfers between devices, mix_the_face(): far_arr = lax.ppermute(far_arr, across, perm=chunks)  85.3 us
    dynamic_update_slice x16, local copies, waits for them, and re-layouts, correlate_plane(): return lax.map(one_group, groups).reshape(-1, 2, PANEL, PANEL)  82.4 us
    dynamic_update_slice x2, local copies, waits for them, and re-layouts, correlate_channels(): return lax.map(one_channel, jnp.moveaxis(turned, 1, 0))  23.3 us
    convert_element_type x1, other arithmetic, on_device(): return (raw / denom[None, :, None, :, :]).astype(jnp.bfloat16)  19.9 us
  transfers between devices with their start and end apart: 16, of which 14 were waited for; matrix products, arithmetic and copies ran while one was open for 1% of the time, Pallas kernels for 0%

profile of v1, /device:TPU:11, one launch (start us, length us, event | category | flops | bytes accessed | tf_op | source)
XLA Modules:
  0.0 724.3 jit_solution(7984971219558250530)
XLA Ops:
  0.7 9.6 %multiply_reduce_fusion = (f32[256]{0:T(256)S(1)}, bf16[256,32,512]{2,0,1:T(8,128)(2,1)}) fusion(bf16[32]{0:T(256)(128)(2,1)S(1)} %exponential_convert_fusion, bf16[256,32,512]{2,1,0:T(8,128)(2,1)} %param.9), kind=kLoop, calls=%fused_computation.29 | loop fusion | flops 16776960 | bytes 16778304 | tf_op jit(solution)/shard_map/reduce_sum | solution.py:45
  18.5 32.6 %collective-permute-done = f32[256]{0:T(256)S(1)} collective-permute-done((f32[256]{0:T(256)S(1)}, f32[256]{0:T(256)S(1)}, u32[]{:S(2)}, u32[]{:S(2)}) %collective-permute-start) | collective-permute-done | bytes 1056 | tf_op jit(solution)/shard_map/ppermute | solution.py:73
  53.5 102.7 %collective-permute-done.1 = f32[256]{0:T(256)S(1)} collective-permute-done((f32[256]{0:T(256)S(1)}, f32[256]{0:T(256)S(1)}, u32[]{:S(2)}, u32[]{:S(2)}) %collective-permute-start.1) | collective-permute-done | bytes 1056 | tf_op jit(solution)/shard_map/ppermute | solution.py:73
  156.2 43.4 %collective-permute-start.2 = (f32[256]{0:T(256)S(1)}, f32[256]{0:T(256)S(1)}, u32[]{:S(2)}, u32[]{:S(2)}) collective-permute-start(f32[256]{0:T(256)S(1)} %collective-permute-done.1), channel_id=1, source_target_pairs={{0,1},{1,2},{2,3},{3,4},{4,5},{5,6},{6,7},{7,8},{8,9},{9,10},{10,1... | collective-permute-start | bytes 3080 | tf_op jit(solution)/shard_map/ppermute | solution.py:73
  256.1 7.5 %copy.26 = bf16[16,256,2,512]{3,1,0,2:T(8,128)(2,1)} copy(bf16[16,256,2,512]{3,1,2,0:T(8,128)(2,1)} %bitcast.3) | data formatting | bytes 16777216 | tf_op jit(solution)/shard_map/all_to_all | solution.py:78
  263.5 440.8 %while.23 = (s32[]{:T(128)}, f32[2,128,2,128,128]{4,3,2,1,0:T(8,128)}, s32[128,2]{0,1:T(2,128)S(1)}, bf16[2,4096,512]{2,1,0:T(8,128)(2,1)}, s32[]{:T(128)}, /*index=5*/s32[]{:T(128)}, s32[]{:T(128)}) while((s32[]{:T(128)}, f32[2,128,2,128,128]{4,3,2,1,0:T(8,128)}, s32[128,2]{0,1:T(2,128)S(1)}, bf16[2,4096,512]{2,1,0:T(8,128)(2,1)}, s32[]{:T(128)}, ...), condition=%wide.region_3.4_spmd, body=%wide.region_0.3_spmd.sunk | while | flops 1348470784 | bytes 138415600 | solution.py:40
  270.5 201.8 %while.24 = (s32[]{:T(128)}, f32[4,32,2,128,128]{4,3,2,1,0:T(8,128)}, s32[4,32,2]{1,0,2:T(4,128)S(1)}, bf16[32,128,512]{2,0,1:T(8,128)(2,1)}, s32[]{:T(128)}) while((s32[]{:T(128)}, f32[4,32,2,128,128]{4,3,2,1,0:T(8,128)}, s32[4,32,2]{1,0,2:T(4,128)S(1)}, bf16[32,128,512]{2,0,1:T(8,128)(2,1)}, s32[]{:T(128)}) %tuple.52), condition=%wide.region_2.2_spmd.clone.clone, body=%wide.region_1.1_spmd.clone.clone.sunk | while | flops 1348470784 | bytes 88081744 | solution.py:32
  276.0 6.9 reshape.101
  288.3 6.9 reshape.102
  295.2 12.5 %fusion.36 = f32[32,2,2,128,128]{3,4,1,2,0:T(8,128)S(1)} fusion(bf16[32,128,2,256,1]{3,2,0,1,4:T(2,128)(2,1)} %bitcast.91, bf16[32,128,2,256,1]{3,2,0,1,4:T(2,128)(2,1)} %bitcast.92), kind=kOutput, calls=%fused_computation.7.clone.1 | convolution fusion | flops 1073741824 | bytes 16777216 | tf_op jit(solution)/shard_map/while/body/eval_jaxpr/while/body/eval_jaxpr/kiat,kjbt->kabij/dot_general | solution.py:27
  326.4 6.9 reshape.101
  338.8 6.9 reshape.102
  345.7 12.5 %fusion.36 = f32[32,2,2,128,128]{3,4,1,2,0:T(8,128)S(1)} fusion(bf16[32,128,2,256,1]{3,2,0,1,4:T(2,128)(2,1)} %bitcast.91, bf16[32,128,2,256,1]{3,2,0,1,4:T(2,128)(2,1)} %bitcast.92), kind=kOutput, calls=%fused_computation.7.clone.1 | convolution fusion | flops 1073741824 | bytes 16777216 | tf_op jit(solution)/shard_map/while/body/eval_jaxpr/while/body/eval_jaxpr/kiat,kjbt->kabij/dot_general | solution.py:27
  376.8 6.9 reshape.101
  396.1 12.5 %fusion.36 = f32[32,2,2,128,128]{3,4,1,2,0:T(8,128)S(1)} fusion(bf16[32,128,2,256,1]{3,2,0,1,4:T(2,128)(2,1)} %bitcast.91, bf16[32,128,2,256,1]{3,2,0,1,4:T(2,128)(2,1)} %bitcast.92), kind=kOutput, calls=%fused_computation.7.clone.1 | convolution fusion | flops 1073741824 | bytes 16777216 | tf_op jit(solution)/shard_map/while/body/eval_jaxpr/while/body/eval_jaxpr/kiat,kjbt->kabij/dot_general | solution.py:27
  427.3 6.9 reshape.101
  439.7 6.9 reshape.102
  446.6 12.5 %fusion.36 = f32[32,2,2,128,128]{3,4,1,2,0:T(8,128)S(1)} fusion(bf16[32,128,2,256,1]{3,2,0,1,4:T(2,128)(2,1)} %bitcast.91, bf16[32,128,2,256,1]{3,2,0,1,4:T(2,128)(2,1)} %bitcast.92), kind=kOutput, calls=%fused_computation.7.clone.1 | convolution fusion | flops 1073741824 | bytes 16777216 | tf_op jit(solution)/shard_map/while/body/eval_jaxpr/while/body/eval_jaxpr/kiat,kjbt->kabij/dot_general | solution.py:27
  472.3 11.6 %bitcast_dynamic-update-slice_fusion.2 = f32[2,128,2,128,128]{4,3,2,1,0:T(8,128)} fusion(f32[2,128,2,128,128]{4,3,2,1,0:T(8,128)} %get-tuple-element.207, s32[]{:T(128)S(6)} %copy.66, f32[1,128,2,128,128]{4,3,2,1,0:T(8,128)} %bitcast.93), kind=kLoop, calls=%fused_computation.26.clone.1 | loop fusion | bytes 33554436 | tf_op jit(solution)/shard_map/while/body/jit(dynamic_update_index_in_dim)/dynamic_update_slice | solution.py:40
  490.9 201.8 %while.24 = (s32[]{:T(128)}, f32[4,32,2,128,128]{4,3,2,1,0:T(8,128)}, s32[4,32,2]{1,0,2:T(4,128)S(1)}, bf16[32,128,512]{2,0,1:T(8,128)(2,1)}, s32[]{:T(128)}) while((s32[]{:T(128)}, f32[4,32,2,128,128]{4,3,2,1,0:T(8,128)}, s32[4,32,2]{1,0,2:T(4,128)S(1)}, bf16[32,128,512]{2,0,1:T(8,128)(2,1)}, s32[]{:T(128)}) %tuple.52), condition=%wide.region_2.2_spmd.clone.clone, body=%wide.region_1.1_spmd.clone.clone.sunk | while | flops 1348470784 | bytes 88081744 | solution.py:32
  496.3 6.9 reshape.101
  515.7 12.5 %fusion.36 = f32[32,2,2,128,128]{3,4,1,2,0:T(8,128)S(1)} fusion(bf16[32,128,2,256,1]{3,2,0,1,4:T(2,128)(2,1)} %bitcast.91, bf16[32,128,2,256,1]{3,2,0,1,4:T(2,128)(2,1)} %bitcast.92), kind=kOutput, calls=%fused_computation.7.clone.1 | convolution fusion | flops 1073741824 | bytes 16777216 | tf_op jit(solution)/shard_map/while/body/eval_jaxpr/while/body/eval_jaxpr/kiat,kjbt->kabij/dot_general | solution.py:27
  546.8 6.9 reshape.101
  559.2 6.9 reshape.102
  566.1 12.5 %fusion.36 = f32[32,2,2,128,128]{3,4,1,2,0:T(8,128)S(1)} fusion(bf16[32,128,2,256,1]{3,2,0,1,4:T(2,128)(2,1)} %bitcast.91, bf16[32,128,2,256,1]{3,2,0,1,4:T(2,128)(2,1)} %bitcast.92), kind=kOutput, calls=%fused_computation.7.clone.1 | convolution fusion | flops 1073741824 | bytes 16777216 | tf_op jit(solution)/shard_map/while/body/eval_jaxpr/while/body/eval_jaxpr/kiat,kjbt->kabij/dot_general | solution.py:27
  597.2 6.9 reshape.101
  609.6 6.9 reshape.102
  616.5 12.5 %fusion.36 = f32[32,2,2,128,128]{3,4,1,2,0:T(8,128)S(1)} fusion(bf16[32,128,2,256,1]{3,2,0,1,4:T(2,128)(2,1)} %bitcast.91, bf16[32,128,2,256,1]{3,2,0,1,4:T(2,128)(2,1)} %bitcast.92), kind=kOutput, calls=%fused_computation.7.clone.1 | convolution fusion | flops 1073741824 | bytes 16777216 | tf_op jit(solution)/shard_map/while/body/eval_jaxpr/while/body/eval_jaxpr/kiat,kjbt->kabij/dot_general | solution.py:27
  647.7 6.9 reshape.101
  667.0 12.5 %fusion.36 = f32[32,2,2,128,128]{3,4,1,2,0:T(8,128)S(1)} fusion(bf16[32,128,2,256,1]{3,2,0,1,4:T(2,128)(2,1)} %bitcast.91, bf16[32,128,2,256,1]{3,2,0,1,4:T(2,128)(2,1)} %bitcast.92), kind=kOutput, calls=%fused_computation.7.clone.1 | convolution fusion | flops 1073741824 | bytes 16777216 | tf_op jit(solution)/shard_map/while/body/eval_jaxpr/while/body/eval_jaxpr/kiat,kjbt->kabij/dot_general | solution.py:27
  692.7 11.6 %bitcast_dynamic-update-slice_fusion.2 = f32[2,128,2,128,128]{4,3,2,1,0:T(8,128)} fusion(f32[2,128,2,128,128]{4,3,2,1,0:T(8,128)} %get-tuple-element.207, s32[]{:T(128)S(6)} %copy.66, f32[1,128,2,128,128]{4,3,2,1,0:T(8,128)} %bitcast.93), kind=kLoop, calls=%fused_computation.26.clone.1 | loop fusion | bytes 33554436 | tf_op jit(solution)/shard_map/while/body/jit(dynamic_update_index_in_dim)/dynamic_update_slice | solution.py:40
  704.3 19.9 %divide_convert_fusion = bf16[2,128,2,128,128]{4,3,2,1,0:T(8,128)(2,1)} fusion(f32[2,128,2,128,128]{4,3,2,1,0:T(8,128)} %get-tuple-element.58, f32[128,128,128]{2,1,0:T(8,128)} %multiply_sqrt_fusion), kind=kLoop, calls=%fused_computation.28 | loop fusion | flops 16777216 | bytes 58720256 | tf_op jit(solution)/shard_map/convert_element_type | solution.py:85
  (141 shorter events, 294.8 us)
Async XLA Ops:
  10.3 8.2 %copy-start = (s32[128,2]{0,1:T(2,128)S(1)}, s32[128,2]{0,1:T(2,128)}, u32[]{:S(2)}) copy-start(s32[128,2]{0,1:T(2,128)} %param.11) | copy-start | bytes 3076
  10.3 245.8 %all-to-all-start = ((bf16[256,32,512]{2,0,1:T(8,128)(2,1)}), bf16[256,32,512]{2,0,1:T(8,128)(2,1)}, u32[]{:S(2)}, u32[]{:S(2)}) async-start(bf16[256,32,512]{2,0,1:T(8,128)(2,1)} %get-tuple-element.112), calls=%async_computation | async-start | bytes 16777216 | tf_op jit(solution)/shard_map/all_to_all | solution.py:78
  17.0 34.0 %collective-permute-start = (f32[256]{0:T(256)S(1)}, f32[256]{0:T(256)S(1)}, u32[]{:S(2)}, u32[]{:S(2)}) collective-permute-start(f32[256]{0:T(256)S(1)} %get-tuple-element.111), channel_id=1, source_target_pairs={{0,1},{1,2},{2,3},{3,4},{4,5},{5,6},{6,7},{7,8},{8,9},{9,10},{10,1... | collective-permute-start | bytes 3080 | tf_op jit(solution)/shard_map/ppermute | solution.py:73
  51.1 105.1 %collective-permute-start.1 = (f32[256]{0:T(256)S(1)}, f32[256]{0:T(256)S(1)}, u32[]{:S(2)}, u32[]{:S(2)}) collective-permute-start(f32[256]{0:T(256)S(1)} %collective-permute-done), channel_id=1, source_target_pairs={{0,1},{1,2},{2,3},{3,4},{4,5},{5,6},{6,7},{7,8},{8,9},{9,10},{10,1... | collective-permute-start | bytes 3080 | tf_op jit(solution)/shard_map/ppermute | solution.py:73
  156.2 44.1 %collective-permute-start.2 = (f32[256]{0:T(256)S(1)}, f32[256]{0:T(256)S(1)}, u32[]{:S(2)}, u32[]{:S(2)}) collective-permute-start(f32[256]{0:T(256)S(1)} %collective-permute-done.1), channel_id=1, source_target_pairs={{0,1},{1,2},{2,3},{3,4},{4,5},{5,6},{6,7},{7,8},{8,9},{9,10},{10,1... | collective-permute-start | bytes 3080 | tf_op jit(solution)/shard_map/ppermute | solution.py:73
  200.3 4.0 collective-permute-start.3
  204.3 3.9 collective-permute-start.4
  208.2 3.9 collective-permute-start.5
  212.1 3.9 collective-permute-start.6
  216.0 3.9 collective-permute-start.7
  219.9 3.9 collective-permute-start.8
  223.8 3.9 collective-permute-start.9
  227.7 3.9 collective-permute-start.10
  231.6 3.9 collective-permute-start.11
  235.5 3.9 collective-permute-start.12
  239.4 3.9 collective-permute-start.13
  243.3 6.5 collective-permute-start.14
